TPU v7x, 128 devices: a whole 4x4x4 slice. The times are simulated.
128 devices in a mesh: dom: 32 (over x, z_lo, y), sub: 4 (over z_hi, core).
Axes of the slice: x: 4, y: 4, z: 4 (z_hi: 2, z_lo: 2; z = z_hi * 2 + z_lo), core: 2. Of those that a mesh axis runs over, the one named last changes fastest.
Arguments:
- features: bfloat16 [65536, 128], P(('dom', 'sub')), may hold values from -6 to 6
- frac: float32 [3, 65536], P(None, ('dom', 'sub')), may hold values from 0 to 1
- k_int: int32 [3, 1024], replicated, may hold values from -6 to 6
- kernel: float32 [1024], replicated, may hold values from 0.05 to 1
- dist: float32 [65536, 64], P(('dom', 'sub')), may hold values from 0.8 to 7
- nbr: int32 [65536, 64], P(('dom', 'sub')), may hold values from 0 to 767, as said below
- send_index: int32 [128, 2, 128], P(('dom', 'sub')), may hold values from 0 to 511, as said below
- counts: int32 [128], P(('dom', 'sub')), may hold values from 256 to 512, as said below
- cot: bfloat16 [65536, 128], P(('dom', 'sub')), may hold values from -6 to 6
- w_msg: bfloat16 [128, 128], replicated, may hold values from -0.5 to 0.5
- w_rad: bfloat16 [16, 128], replicated, may hold values from -1.5 to 1.5
- w_q: bfloat16 [128, 128], replicated, may hold values from -0.5 to 0.5
- w_o: bfloat16 [128, 128], replicated, may hold values from -0.5 to 0.5
Outputs:
- grad_features: float32 [65536, 128], P(('dom', 'sub'))
- grad_w_msg: float32 [128, 128], replicated
- grad_w_rad: float32 [16, 128], replicated
- grad_w_q: float32 [128, 128], replicated
- grad_w_o: float32 [128, 128], replicated
Inputs may be any that keep to these rules, and one draw needn't show every extreme that they name: One device has counts = 512. `nbr`: a slot value below 512 names a local row below the device's count (a live atom); a slot r >= 512 names ghost row r - 512 of ext; the slots of local rows b * 128 to (b + 1) * 128 - 1 name ghost rows or local rows w to w + 255, with w = min(max(b * 128 - 128 // 2, 0), 256). `send_index`: every entry is below the device's count; entries may repeat.
All inputs are finite; a program needn't handle non-finite values.
Results may differ from a plain program's by a relative error of at most 0.0061.
Values may be sent and summed in bfloat16 or wider, within the bound.
A program may use at most 64 MiB of HBM per device.

v0:
```python
import math

import jax
import jax.numpy as jnp
import numpy as np
from jax import lax
from jax.experimental import pallas as pl
from jax.experimental.pallas import tpu as pltpu
from jax.sharding import PartitionSpec as P

MESH = pl.DeviceIdType.MESH
BF = jnp.bfloat16
F32 = jnp.float32

WIDTH, GHOSTS, CHANS, SLOTS, KCOUNT, NB = 512, 128, 128, 64, 1024, 16
BLOCK, WINDOW = 128, 256
X, YZ, CORES = 4, 16, 2
HALF, QUART, PIECE = KCOUNT, KCOUNT // X, KCOUNT // X // YZ
TOTAL = WIDTH * X * YZ * CORES
ROWS_AR = 24


def fitted(fn, degree):
    nodes = (np.cos(np.pi * (np.arange(64) + 0.5) / 64) + 1.0) / 8.0
    series = np.polynomial.chebyshev.Chebyshev.fit(nodes, fn(nodes), degree, domain=[0.0, 0.25])
    return [float(np.float32(c)) for c in series.convert(kind=np.polynomial.Polynomial).coef]


COS = fitted(lambda y: np.cos(2 * np.pi * np.sqrt(y)), 7)
SIN = fitted(lambda y: np.sin(2 * np.pi * np.sqrt(y)) / np.sqrt(y), 6)


def horner(coefs, y):
    value = coefs[-1] * y + coefs[-2]
    for c in coefs[-3::-1]:
        value = value * y + c
    return value


def tn(a, b):
    return lax.dot_general(a, b, (((0,), (0,)), ((), ())), preferred_element_type=F32)


def nt(a, b):
    return lax.dot_general(a, b, (((1,), (1,)), ((), ())), preferred_element_type=F32)


def nn(a, b):
    return jnp.dot(a, b, preferred_element_type=F32)


def transposed(a):
    return jnp.transpose(a.astype(F32)).astype(a.dtype)


def kernel(
    feat, frac, kint, kern, dist, nbr, send, counts, cot, wmsg, wrad, wq, wo,
    gf_out, gmsg_out, rad_out, gwq_out, gwo_out,
    table, sg, sg_b, rc, xs, xs_b, rx, ys, ys_b, ry, ag, pc_t,
    g_b, place_t, out_b, ghost, u_own, u_ghost,
    dz, env, lo_s, code_s, gmat, ymat, gul, gug, radacc, gh_b, back, p_t,
    ar, ar1, ar2, fin, send_sem, recv_sem,
):
    dom, sub = lax.axis_index("dom"), lax.axis_index("sub")
    x, inner = dom // 8, dom % 8
    zhi, core = sub // 2, sub % 2
    yz = inner * 2 + zhi
    flat = dom * 4 + sub

    def by_flat(d):
        return (d // 4, d % 4)

    def by_yz(o):
        idx = (yz + o) % YZ
        return idx, (x * 8 + idx // 2, (idx % 2) * 2 + core)

    def by_x(o):
        idx = (x + o) % X
        return idx, (idx * 8 + inner, sub)

    def by_xc(o):
        idx = (x * 2 + core + o) % 8
        return (idx // 2 * 8 + inner, zhi * 2 + idx % 2)

    other_core = (dom, zhi * 2 + 1 - core)
    upper, lower = by_flat((flat + 1) % 128), by_flat((flat + 127) % 128)

    barrier = pltpu.get_barrier_semaphore()
    greeted = [upper, lower, other_core]
    greeted += [by_x(o)[1] for o in range(1, X)]
    greeted += [by_yz(o)[1] for o in range(1, YZ)]
    greeted += [by_xc(o) for o in (1, 3, 5, 7)]
    greeted += [by_xc(o) for o in (2, 4, 6)]
    for peer in greeted:
        pl.semaphore_signal(barrier, inc=1, device_id=peer, device_id_type=MESH)

    sems = iter(range(128))

    def copy(src, dst, peer):
        at = next(sems)
        return pltpu.make_async_remote_copy(
            src_ref=src, dst_ref=dst, send_sem=send_sem.at[at], recv_sem=recv_sem.at[at],
            device_id=peer, device_id_type=MESH,
        )

    live = lax.broadcasted_iota(jnp.int32, (WIDTH, CHANS), 0) < counts[0]
    g_b[...] = jnp.where(live, cot[...].astype(F32), 0.0).astype(BF)
    picks = jnp.concatenate([send[0:1, :], send[1:2, :]], axis=1)
    place_t[...] = jnp.where(
        lax.broadcasted_iota(jnp.int32, (WIDTH, 2 * GHOSTS), 0) == picks, 1.0, 0.0
    ).astype(BF)
    out_b[...] = tn(place_t[...], feat[...]).astype(BF)

    def table_rows(step, _):
        base = pl.multiple_of(step * 128, 128)
        k_real = kint[:, pl.ds(base, 128)].astype(F32)
        for part in range(4):
            cols = slice(part * 128, part * 128 + 128)
            turns = lax.dot_general(
                k_real, frac[:, cols], (((0,), (0,)), ((), ())),
                precision=lax.Precision.HIGHEST, preferred_element_type=F32,
            )
            turns = turns - jnp.floor(turns + 0.5)
            square = turns * turns
            table[pl.ds(base, 128), cols] = horner(COS, square).astype(BF)
            table[pl.ds(KCOUNT + base, 128), cols] = (horner(SIN, square) * turns).astype(BF)
        return 0

    lax.fori_loop(0, KCOUNT // 128, table_rows, 0)

    def sg_rows(step, _):
        rows = pl.ds(pl.multiple_of(step * 256, 256), 256)
        part = nn(table[rows, :], g_b[...])
        sg[rows, :] = part
        sg_b[rows, :] = part.astype(BF)
        return 0

    lax.fori_loop(0, 2 * KCOUNT // 256, sg_rows, 0)

    pl.semaphore_wait(barrier, len(greeted))

    halo = [
        copy(out_b.at[pl.ds(0, GHOSTS)], ghost.at[pl.ds(GHOSTS, GHOSTS)], lower),
        copy(out_b.at[pl.ds(GHOSTS, GHOSTS)], ghost.at[pl.ds(0, GHOSTS)], upper),
    ]
    cores = copy(sg_b.at[pl.ds(pl.multiple_of((1 - core) * HALF, HALF), HALF)], rc, other_core)
    for c in halo + [cores]:
        c.start()

    def spread_block(blk):
        w = min(max(blk * BLOCK - BLOCK // 2, 0), WIDTH - WINDOW)
        half = BLOCK // 2
        first, second = slice(blk * BLOCK, blk * BLOCK + half), slice(blk * BLOCK + half, (blk + 1) * BLOCK)
        d2 = jnp.concatenate([dist[first, :], dist[second, :]], axis=1)
        n2 = jnp.concatenate([nbr[first, :], nbr[second, :]], axis=1)
        dz[...] = d2 * (1.0 / 0.4)
        env[...] = jnp.square(jnp.maximum(0.0, 1.0 - d2 * (1.0 / 6.0)))
        place = jnp.where(n2 >= WIDTH, n2 - (WIDTH - WINDOW), n2 - w)
        lane = lax.broadcasted_iota(jnp.int32, (half, 128), 1)
        lo_s[...] = (place & 127).astype(F32)
        code_s[...] = ((place >> 7) + jnp.where(lane >= SLOTS, 4, 0)).astype(F32)

        def group(step, _):
            base = pl.multiple_of(step * 8, 8)
            rows = pl.ds(base, 8)
            dz8, env8, lo8, code8 = dz[rows, :], env[rows, :], lo_s[rows, :], code_s[rows, :]
            b_ids = lax.broadcasted_iota(jnp.int32, (NB, 128), 0).astype(F32)
            lo_ids = lax.broadcasted_iota(jnp.int32, (128, 128), 0).astype(F32).astype(BF)
            for s in range(8):
                z = dz8[s : s + 1, :] - b_ids
                basis = (jnp.exp(-(z * z)) * env8[s : s + 1, :]).astype(BF)
                code = jnp.broadcast_to(code8[s : s + 1, :], (NB, 128)).astype(BF)
                lhs = jnp.concatenate(
                    [jnp.where(code == h, basis, jnp.zeros_like(basis)) for h in range(8)], axis=0
                )
                lo = jnp.broadcast_to(lo8[s : s + 1, :], (128, 128)).astype(BF)
                hot = jnp.where(lo_ids == lo, jnp.ones_like(lo), jnp.zeros_like(lo))
                out = nt(lhs, hot).astype(BF)
                for i in range(2):
                    at = pl.multiple_of((blk * BLOCK + i * half + s) * NB + base * NB, NB)
                    for h in range(4):
                        r = (i * 4 + h) * NB
                        gmat[pl.ds(at, NB), h * 128 : h * 128 + 128] = out[r : r + NB, :]
            return 0

        lax.fori_loop(0, half // 8, group, 0)

    spread_block(0)

    cores.wait()
    mine = pl.multiple_of(core * HALF, HALF)

    def add_core(step, _):
        rows = pl.ds(pl.multiple_of(step * 128, 128), 128)
        val = sg[pl.ds(pl.multiple_of(mine + step * 128, 128), 128), :] + rc[rows, :].astype(F32)
        xs[rows, :] = val
        xs_b[rows, :] = val.astype(BF)
        return 0

    lax.fori_loop(0, HALF // 128, add_core, 0)
    along_x = []
    for o in range(1, X):
        idx, peer = by_x(o)
        along_x.append(copy(xs_b.at[pl.ds(pl.multiple_of(idx * QUART, QUART), QUART)], rx.at[o - 1], peer))
    for c in along_x:
        c.start()

    spread_block(1)

    for c in along_x:
        c.wait()
    val = xs[pl.ds(pl.multiple_of(x * QUART, QUART), QUART), :]
    for o in range(1, X):
        val = val + rx[o - 1].astype(F32)
    ys[...] = val
    ys_b[...] = val.astype(BF)
    along_yz = []
    for o in range(1, YZ):
        idx, peer = by_yz(o)
        along_yz.append(copy(ys_b.at[pl.ds(pl.multiple_of(idx * PIECE, PIECE), PIECE)], ry.at[o - 1], peer))
    for c in along_yz:
        c.start()

    spread_block(2)

    for c in along_yz:
        c.wait()
    val = ys[pl.ds(pl.multiple_of(yz * PIECE, PIECE), PIECE), :]
    for o in range(1, YZ):
        val = val + ry[o - 1].astype(F32)
    at_piece = pl.ds(pl.multiple_of(core * HALF + x * QUART + yz * PIECE, PIECE), PIECE)
    at_quart = pl.ds(pl.multiple_of(core * HALF + x * QUART, QUART), QUART)
    at_half = pl.ds(mine, HALF)
    ag[at_piece, :] = val.astype(BF)
    gather_yz = [copy(ag.at[at_piece], ag.at[at_piece], by_yz(o)[1]) for o in range(1, YZ)]
    for c in gather_yz:
        c.start()

    spread_block(3)

    for c in gather_yz:
        c.wait()
    gather_x = [copy(ag.at[at_quart], ag.at[at_quart], by_x(o)[1]) for o in range(1, X)]
    for c in gather_x:
        c.start()

    for c in halo:
        c.wait()
    u_own[...] = nn(feat[...], wmsg[...]).astype(BF)
    u_ghost[...] = nn(ghost[...], wmsg[...]).astype(BF)
    gul[...] = jnp.zeros_like(gul)
    gug[...] = jnp.zeros_like(gug)
    radacc[...] = jnp.zeros_like(radacc)
    wr = wrad[...].astype(F32)

    def edge_block(blk, _):
        w = pl.multiple_of(jnp.clip(blk * BLOCK - BLOCK // 2, 0, WIDTH - WINDOW), 64)
        u_win = u_own[pl.ds(w, WINDOW), :]
        ug = u_ghost[...]
        piece = 32

        def atoms(step, _):
            at = pl.multiple_of(blk * BLOCK + step * piece, piece)
            rows = pl.ds(pl.multiple_of(at * NB, NB * piece), NB * piece)
            summed = nn(gmat[rows, :WINDOW], u_win) + nn(gmat[rows, WINDOW:], ug)
            summed = summed.reshape(piece, NB, CHANS)
            pre = jnp.sum(summed * wr[None], axis=1)
            sig = 1.0 / (1.0 + jnp.exp(-pre))
            gpre = g_b[pl.ds(at, piece), :].astype(F32) * sig * (1.0 + pre * (1.0 - sig))
            wide = gpre[:, None, :]
            radacc[...] += jnp.sum(wide * summed, axis=0)
            ymat[pl.ds(pl.multiple_of(step * piece * NB, NB * piece), NB * piece), :] = (
                (wide * wr[None]).reshape(piece * NB, CHANS).astype(BF)
            )
            return 0

        lax.fori_loop(0, BLOCK // piece, atoms, 0)
        rows = pl.ds(pl.multiple_of(blk * BLOCK * NB, BLOCK * NB), BLOCK * NB)
        collected = jnp.transpose(tn(ymat[...], gmat[rows, :]))
        gul[pl.ds(w, WINDOW), :] += collected[:WINDOW, :]
        gug[...] += collected[WINDOW:, :]
        return 0

    edge_block(0, 0)
    for c in gather_x:
        c.wait()
    gather_core = copy(ag.at[at_half], ag.at[at_half], other_core)
    gather_core.start()
    lax.fori_loop(1, WIDTH // BLOCK, edge_block, 0)

    gu_g = gug[...].astype(BF)
    gu_l = gul[...].astype(BF)
    gh_b[...] = nt(gu_g, wmsg[...]).astype(BF)
    returns = [
        copy(gh_b.at[pl.ds(0, GHOSTS)], back.at[pl.ds(GHOSTS, GHOSTS)], lower),
        copy(gh_b.at[pl.ds(GHOSTS, GHOSTS)], back.at[pl.ds(0, GHOSTS)], upper),
    ]
    for c in returns:
        c.start()
    gmsg = tn(feat[...], gu_l) + tn(ghost[...], gu_g)

    gather_core.wait()

    def flip(step, _):
        base = pl.multiple_of(step * 128, 128)
        weight = kern[:, pl.ds(pl.multiple_of((step % 8) * 128, 128), 128)]
        part = jnp.transpose(ag[pl.ds(base, 128), :].astype(F32))
        pc_t[:, pl.ds(base, 128)] = (part * (weight * (1.0 / math.sqrt(KCOUNT * TOTAL)))).astype(BF)
        return 0

    lax.fori_loop(0, 2 * KCOUNT // 128, flip, 0)
    p_t[...] = nn(pc_t[...], table[...]).astype(BF)
    f_live = jnp.where(live, feat[...].astype(F32), 0.0).astype(BF)
    m_t = nn(p_t[...], f_live)

    ar[:, 0:8, :] = gmsg.reshape(YZ, 8, CHANS)
    ar[:, 8:16, :] = m_t.reshape(YZ, 8, CHANS)
    ar[:, 16:24, :] = jnp.zeros((YZ, 8, CHANS), F32)
    for j in range(YZ):
        ar[j, 16:17, :] = radacc[j : j + 1, :]
    ar_yz = []
    for o in range(1, YZ):
        idx, peer = by_yz(o)
        ar_yz.append(copy(ar.at[idx], ar1.at[o - 1], peer))
    for c in ar_yz:
        c.start()

    gq_t = nn(wo[...], p_t[...]).astype(BF)
    ghq = jnp.transpose(nn(wq[...], gq_t))
    base_grad = g_b[...].astype(F32) + nt(gu_l, wmsg[...]) + jnp.where(live, ghq, 0.0)
    for c in returns:
        c.wait()
    gf_out[...] = base_grad + nn(place_t[...], back[...])

    for c in ar_yz:
        c.wait()
    val = ar[yz]
    for o in range(1, YZ):
        val = val + ar1[o - 1]
    me = x * 2 + core
    ar2[me] = val
    ar_xc = [copy(ar2.at[me], ar2.at[me], by_xc(o)) for o in range(1, 8)]
    for c in ar_xc:
        c.start()
    for c in ar_xc:
        c.wait()
    val = ar2[0]
    for j in range(1, 8):
        val = val + ar2[j]
    fin[yz] = val
    ar_fin = [copy(fin.at[yz], fin.at[yz], by_yz(o)[1]) for o in range(1, YZ)]
    for c in ar_fin:
        c.start()
    for c in ar_fin:
        c.wait()

    rscale = 1.0 / math.sqrt(TOTAL)
    gmsg_out[...] = fin[:, 0:8, :].reshape(CHANS, CHANS) * rscale
    for j in range(NB):
        rad_out[j : j + 1, :] = fin[j, 16:17, :] * (rscale / math.sqrt(SLOTS))
    m_full = jnp.transpose(fin[:, 8:16, :].reshape(CHANS, CHANS))
    m_hi = m_full.astype(BF)
    m_lo = (m_full - m_hi.astype(F32)).astype(BF)
    gwq_out[...] = (nt(m_hi, wo[...]) + nt(m_lo, wo[...])) * rscale
    wq_t = transposed(wq[...])
    gwo_out[...] = (nn(wq_t, m_hi) + nn(wq_t, m_lo)) * rscale


def on_device(features, frac, k_int, kern, dist, nbr, send_index, counts, cot, w_msg, w_rad, w_q, w_o):
    vmem = pl.BlockSpec(memory_space=pltpu.VMEM)
    smem = pl.BlockSpec(memory_space=pltpu.SMEM)

    def buf(*shape, dtype=BF):
        return pltpu.VMEM(shape, dtype)

    return pl.pallas_call(
        kernel,
        out_shape=(
            jax.ShapeDtypeStruct((WIDTH, CHANS), F32),
            jax.ShapeDtypeStruct((CHANS, CHANS), F32),
            jax.ShapeDtypeStruct((NB, CHANS), F32),
            jax.ShapeDtypeStruct((CHANS, CHANS), F32),
            jax.ShapeDtypeStruct((CHANS, CHANS), F32),
        ),
        in_specs=[vmem] * 7 + [smem] + [vmem] * 5,
        out_specs=(vmem,) * 5,
        scratch_shapes=[
            buf(2 * KCOUNT, WIDTH),
            buf(2 * KCOUNT, CHANS, dtype=F32),
            buf(2 * KCOUNT, CHANS),
            buf(HALF, CHANS),
            buf(HALF, CHANS, dtype=F32),
            buf(HALF, CHANS),
            buf(X - 1, QUART, CHANS),
            buf(QUART, CHANS, dtype=F32),
            buf(QUART, CHANS),
            buf(YZ - 1, PIECE, CHANS),
            buf(2 * KCOUNT, CHANS),
            buf(CHANS, 2 * KCOUNT),
            buf(WIDTH, CHANS),
            buf(WIDTH, 2 * GHOSTS),
            buf(2 * GHOSTS, CHANS),
            buf(2 * GHOSTS, CHANS),
            buf(WIDTH, CHANS),
            buf(2 * GHOSTS, CHANS),
            buf(BLOCK // 2, 128, dtype=F32),
            buf(BLOCK // 2, 128, dtype=F32),
            buf(BLOCK // 2, 128, dtype=F32),
            buf(BLOCK // 2, 128, dtype=F32),
            buf(WIDTH * NB, 2 * WINDOW),
            buf(BLOCK * NB, CHANS),
            buf(WIDTH, CHANS, dtype=F32),
            buf(2 * GHOSTS, CHANS, dtype=F32),
            buf(NB, CHANS, dtype=F32),
            buf(2 * GHOSTS, CHANS),
            buf(2 * GHOSTS, CHANS),
            buf(CHANS, WIDTH),
            buf(YZ, ROWS_AR, CHANS, dtype=F32),
            buf(YZ - 1, ROWS_AR, CHANS, dtype=F32),
            buf(8, ROWS_AR, CHANS, dtype=F32),
            buf(YZ, ROWS_AR, CHANS, dtype=F32),
            pltpu.SemaphoreType.DMA((96,)),
            pltpu.SemaphoreType.DMA((96,)),
        ],
        compiler_params=pltpu.CompilerParams(
            collective_id=0, has_side_effects=True, vmem_limit_bytes=48 * 1024 * 1024
        ),
        name="ewald_backward",
    )(
        features, frac, k_int, kern.reshape(1, KCOUNT), dist, nbr,
        send_index.reshape(2, GHOSTS), counts, cot, w_msg, w_rad, w_q, w_o,
    )


def solution(mesh):
    rows = P(("dom", "sub"), None)
    placed = (
        rows, P(None, ("dom", "sub")), P(), P(), rows, rows,
        P(("dom", "sub"), None, None), P(("dom", "sub")), rows, P(), P(), P(), P(),
    )
    return jax.shard_map(
        on_device,
        mesh=mesh,
        in_specs=placed,
        out_specs=(rows, P(), P(), P(), P()),
        check_vma=False,
    )
```

profile of v0, /device:TPU:1, one launch (start us, length us, event | category | flops | bytes accessed | tf_op | source)
XLA Modules:
  0.0 66.6 jit_solution(4798226568466081611)
XLA Ops:
  1.3 1.1 %copy.18.dist = f32[512,64]{1,0:T(8,128)S(1)} copy(f32[512,64]{0,1:T(8,128)} %param.17) | data formatting | bytes 262144 | tf_op args[4]
  2.4 0.0 copy-done.10
  2.4 0.0 copy-start
  2.4 0.0 copy-start.1
  2.4 0.0 copy-start.2
  2.4 0.0 copy-start.3
  2.4 0.0 copy-start.4
  2.4 0.0 copy-start.5
  2.4 0.0 copy-start.6
  2.5 0.0 copy-start.7
  2.5 0.0 copy-start.8
  2.5 0.1 copy.19.nbr
  2.6 0.7 copy-done
  3.3 0.1 copy-done.1
  3.3 0.0 copy-done.2
  3.4 0.0 copy-done.6
  3.4 0.0 copy-done.7
  3.4 0.0 copy-done.8
  3.4 60.0 %ewald_backward.1 = (f32[512,128]{1,0:T(8,128)S(1)}, f32[128,128]{1,0:T(8,128)S(1)}, f32[16,128]{1,0:T(8,128)S(1)}, f32[128,128]{1,0:T(8,128)S(1)}, f32[128,128]{1,0:T(8,128)S(1)}) custom-call(bf16[512,128]{1,0:T(8,128)(2,1)S(1)} %copy-done, f32[3,512]{1,0:T(4,128)S(1)} %copy-done.6, s32[3,1024]{1,0:T(4,128)S(1)} %copy-done.5, f32[1,1024]{1,0:T(1,128)S(1)} %bitcast.2, ...), custom_call_target="tpu_custom_call" | custom-call | tf_op jit(solution)/shard_map/ewald_backward/pallas_call | solution.py:376
  63.4 0.7 %copy.26 = f32[512,128]{1,0:T(8,128)} copy(f32[512,128]{1,0:T(8,128)S(1)} %get-tuple-element.10) | data formatting | bytes 524288
  64.1 0.6 copy.27
  64.7 0.6 copy.28
  65.3 0.6 copy.29
  65.9 0.6 copy.30
  (6 shorter events, 0.0 us)
Async XLA Ops:
  1.3 1.1 %copy-start.10 = (s32[512,64]{0,1:T(8,128)S(1)}, s32[512,64]{0,1:T(8,128)}, u32[]{:S(2)}) copy-start(s32[512,64]{0,1:T(8,128)} %param.18) | copy-start | bytes 393220
  1.3 1.3 %copy-start.9 = (s32[1,2,128]{2,1,0:T(2,128)S(1)}, s32[1,2,128]{2,1,0:T(2,128)}, u32[]{:S(2)}) copy-start(s32[1,2,128]{2,1,0:T(2,128)} %param.19) | copy-start | bytes 3076
  2.4 0.9 %copy-start = (bf16[512,128]{1,0:T(8,128)(2,1)S(1)}, bf16[512,128]{1,0:T(8,128)(2,1)}, u32[]{:S(2)}) copy-start(bf16[512,128]{1,0:T(8,128)(2,1)} %feat.1) | copy-start | bytes 393220
  2.4 1.0 %copy-start.1 = (bf16[512,128]{1,0:T(8,128)(2,1)S(1)}, bf16[512,128]{1,0:T(8,128)(2,1)}, u32[]{:S(2)}) copy-start(bf16[512,128]{1,0:T(8,128)(2,1)} %cot.1) | copy-start | bytes 393220
  2.4 1.0 %copy-start.2 = (bf16[128,128]{1,0:T(8,128)(2,1)S(1)}, bf16[128,128]{1,0:T(8,128)(2,1)}, u32[]{:S(2)}) copy-start(bf16[128,128]{1,0:T(8,128)(2,1)} %wmsg.1) | copy-start | bytes 98308
  2.4 0.9 %copy-start.3 = (bf16[128,128]{1,0:T(8,128)(2,1)S(1)}, bf16[128,128]{1,0:T(8,128)(2,1)}, u32[]{:S(2)}) copy-start(bf16[128,128]{1,0:T(8,128)(2,1)} %wq.1) | copy-start | bytes 98308
  2.4 0.9 %copy-start.4 = (bf16[128,128]{1,0:T(8,128)(2,1)S(1)}, bf16[128,128]{1,0:T(8,128)(2,1)}, u32[]{:S(2)}) copy-start(bf16[128,128]{1,0:T(8,128)(2,1)} %wo.1) | copy-start | bytes 98308
  2.4 0.9 %copy-start.5 = (s32[3,1024]{1,0:T(4,128)S(1)}, s32[3,1024]{1,0:T(4,128)}, u32[]{:S(2)}) copy-start(s32[3,1024]{1,0:T(4,128)} %kint.1) | copy-start | bytes 36868
  2.4 0.9 %copy-start.6 = (f32[3,512]{1,0:T(4,128)S(1)}, f32[3,512]{1,0:T(4,128)}, u32[]{:S(2)}) copy-start(f32[3,512]{1,0:T(4,128)} %frac.1) | copy-start | bytes 18436
  2.5 0.9 %copy-start.7 = (f32[1024]{0:T(1024)S(1)}, f32[1024]{0:T(1024)}, u32[]{:S(2)}) copy-start(f32[1024]{0:T(1024)} %param.16) | copy-start | bytes 12292
  2.5 0.9 %copy-start.8 = (bf16[16,128]{1,0:T(8,128)(2,1)S(1)}, bf16[16,128]{1,0:T(8,128)(2,1)}, u32[]{:S(2)}) copy-start(bf16[16,128]{1,0:T(8,128)(2,1)} %wrad.1) | copy-start | bytes 12292
where the time goes:
time: 66.7 us; the launch traced here: 66.6 us
  Pallas kernels  60 us (90%)
  local copies, waits for them, and re-layouts  5.16 us (8%)
  between operations  1.44 us (2%)
    pallas_call x1, Pallas kernels, on_device(): pl.pallas_call(kernel, out_shape=(jax.ShapeDtypeStruct((WIDTH, CHANS), F3...  60 us
    unnamed x29, local copies, waits for them, and re-layouts  5.16 us

commit v1 on v0

v1 whole, which is shorter than its diff:
```python
import math

import jax
import jax.numpy as jnp
import numpy as np
from jax import lax
from jax.experimental import pallas as pl
from jax.experimental.pallas import tpu as pltpu
from jax.sharding import PartitionSpec as P

MESH = pl.DeviceIdType.MESH
BF = jnp.bfloat16
F32 = jnp.float32

WIDTH, GHOSTS, CHANS, SLOTS, KCOUNT, NB = 512, 128, 128, 64, 1024, 16
BLOCK, WINDOW = 128, 256
X, YZ, CORES = 4, 16, 2
CHIPS = X * YZ
PIECE = KCOUNT // CHIPS
TOTAL = WIDTH * CHIPS * CORES
BOTH = 2 * CHANS
ROWS_AR = 24
VMEM_BYTES = 63 * 1024 * 1024


def fitted(fn, degree):
    nodes = (np.cos(np.pi * (np.arange(64) + 0.5) / 64) + 1.0) / 8.0
    series = np.polynomial.chebyshev.Chebyshev.fit(nodes, fn(nodes), degree, domain=[0.0, 0.25])
    return [float(np.float32(c)) for c in series.convert(kind=np.polynomial.Polynomial).coef]


COS = fitted(lambda y: np.cos(2 * np.pi * np.sqrt(y)), 6)
SIN = fitted(lambda y: np.sin(2 * np.pi * np.sqrt(y)) / np.sqrt(y), 5)


def horner(coefs, y):
    value = coefs[-1] * y + coefs[-2]
    for c in coefs[-3::-1]:
        value = value * y + c
    return value


def tn(a, b):
    return lax.dot_general(a, b, (((0,), (0,)), ((), ())), preferred_element_type=F32)


def nt(a, b):
    return lax.dot_general(a, b, (((1,), (1,)), ((), ())), preferred_element_type=F32)


def nn(a, b):
    return jnp.dot(a, b, preferred_element_type=F32)


def transposed(a):
    return jnp.transpose(a.astype(F32)).astype(a.dtype)


def kernel(
    feat_h, frac_h, kint_h, kern_h, dist_h, nbr_h, send_h, counts_h, cot_h, wmsg_h, wrad_h, wq_h, wo_h,
    gf_out, gmsg_out, rad_out, gwq_out, gwo_out,
    feat, frac, kint, kern, dist, nbr, send, counts, cot, wmsg, wrad, wq, wo,
    gf, gmsg_s, rad_s, gwq, gwo,
    table, sg_b, rc, xs, xs_b, rx, ag, pc_t,
    fg, place_t, out_b, ghost, u_own, u_ghost,
    dz, env, lo_s, code_s, gmat, ymat, gul, gug, radacc, gh_b, back, p_t, m_s,
    ar, ar1, ar2, fin, in_sem, out_sem, send_sem, recv_sem, rs_send, rs_recv, ag_send, ag_recv,
):
    dom, sub = lax.axis_index("dom"), lax.axis_index("sub")
    x, zlo, y = dom // 8, (dom // 4) % 2, dom % 4
    zhi, core = sub // 2, sub % 2
    z = zhi * 2 + zlo
    yz = y * 4 + z
    chip = x * YZ + yz
    flat = dom * 4 + sub

    px = [(x + d) % 4 for d in range(4)]
    py = [(y + d) % 4 for d in range(4)]
    pz = [(z + d) % 4 for d in range(4)]
    far = [p * 8 for p in px]
    along = [(p % 2) * 4 for p in pz]
    pair_of = [(p // 2) * 2 for p in pz]
    both_cores = [core, 1 - core]

    def shifted(dx, dy, dz_, dc=0):
        where = (far[dx] + (along[dz_] + py[dy]), pair_of[dz_] + both_cores[dc])
        return px[dx] * YZ + (py[dy] * 4 + pz[dz_]), where

    def hops(turn):
        return sum(min(d, 4 - d) for d in turn)

    turns = [(a, b, c) for a in range(4) for b in range(4) for c in range(4) if a or b or c]
    turns = sorted(turns, key=lambda t: -hops(t))
    places = [shifted(*t) for t in turns]
    plane = [(t, p) for t, p in zip(turns, places) if not t[0]]

    other_core = (dom, zhi * 2 + 1 - core)
    upper, lower = (flat + 1) % 128, (flat + 127) % 128
    upper, lower = (upper // 4, upper % 4), (lower // 4, lower % 4)
    across = [(dx, dc) for dx in (2, 1, 3, 0) for dc in (1, 0) if dx or dc]
    across = [shifted(dx, 0, 0, dc)[1] for dx, dc in across]

    barrier = pltpu.get_barrier_semaphore()

    def greet(peer):
        pl.semaphore_signal(barrier, inc=1, device_id=peer, device_id_type=MESH)

    for _, peer in places:
        greet(peer)
    for peer in (upper, lower, other_core):
        greet(peer)
    for dx in range(1, X):
        greet(shifted(dx, 0, 0, 1)[1])
    greeted = CHIPS - 1 + 3 + X - 1

    sems = iter(range(128))

    def copy(src, dst, peer):
        at = next(sems)
        return pltpu.make_async_remote_copy(
            src_ref=src, dst_ref=dst, send_sem=send_sem.at[at], recv_sem=recv_sem.at[at],
            device_id=peer, device_id_type=MESH,
        )

    pairs = [
        (counts_h, counts), (kint_h, kint), (frac_h, frac), (feat_h, feat), (cot_h, cot), (send_h, send),
        (dist_h, dist), (nbr_h, nbr), (wmsg_h, wmsg), (wrad_h, wrad), (kern_h, kern), (wq_h, wq), (wo_h, wo),
    ]
    loads = [pltpu.make_async_copy(src, dst, in_sem.at[i]) for i, (src, dst) in enumerate(pairs)]
    for c in loads:
        c.start()
    for c in loads:
        c.wait()

    live = lax.broadcasted_iota(jnp.int32, (WIDTH, CHANS), 0) < counts[0]
    fg[:, :CHANS] = jnp.where(live, feat[...].astype(F32), 0.0).astype(BF)
    fg[:, CHANS:] = jnp.where(live, cot[...].astype(F32), 0.0).astype(BF)
    picks = jnp.concatenate([send[0:1, :], send[1:2, :]], axis=1)
    place_t[...] = jnp.where(
        lax.broadcasted_iota(jnp.int32, (WIDTH, 2 * GHOSTS), 0) == picks, 1.0, 0.0
    ).astype(BF)
    out_b[...] = tn(place_t[...], feat[...]).astype(BF)

    def table_rows(step, _):
        base = pl.multiple_of(step * 128, 128)
        k_real = kint[:, pl.ds(base, 128)].astype(F32)
        for part in range(4):
            cols = slice(part * 128, part * 128 + 128)
            turns = lax.dot_general(
                k_real, frac[:, cols], (((0,), (0,)), ((), ())),
                precision=lax.Precision.HIGHEST, preferred_element_type=F32,
            )
            turns = turns - jnp.floor(turns + 0.5)
            square = turns * turns
            table[pl.ds(base, 128), cols] = horner(COS, square).astype(BF)
            table[pl.ds(KCOUNT + base, 128), cols] = (horner(SIN, square) * turns).astype(BF)
        return 0

    lax.fori_loop(0, KCOUNT // 128, table_rows, 0)

    theirs = pl.multiple_of((1 - core) * KCOUNT, KCOUNT)
    mine = pl.multiple_of(core * KCOUNT, KCOUNT)
    sg_b[...] = nn(table[pl.ds(theirs, KCOUNT), :], fg[...]).astype(BF)
    xs[...] = nn(table[pl.ds(mine, KCOUNT), :], fg[...])

    pl.semaphore_wait(barrier, greeted)

    halo = [
        copy(out_b.at[pl.ds(0, GHOSTS)], ghost.at[pl.ds(GHOSTS, GHOSTS)], lower),
        copy(out_b.at[pl.ds(GHOSTS, GHOSTS)], ghost.at[pl.ds(0, GHOSTS)], upper),
    ]
    cores = copy(sg_b, rc, other_core)
    for c in [cores] + halo:
        c.start()

    def spread_setup(pair):
        blocks = (2 * pair, 2 * pair + 1)
        d_parts, p_parts = [], []
        for i, blk in enumerate(blocks):
            w = min(max(blk * BLOCK - BLOCK // 2, 0), WIDTH - WINDOW)
            cols = slice(blk * BLOCK, (blk + 1) * BLOCK)
            n = nbr[:, cols]
            d_parts.append(dist[:, cols])
            place = jnp.where(n >= WIDTH, n - (WIDTH - WINDOW), n - w) + i * 2 * WINDOW
            p_parts.append(place.astype(F32))
        d2 = jnp.transpose(jnp.concatenate(d_parts, axis=0))
        place = jnp.transpose(jnp.concatenate(p_parts, axis=0))
        dz[...] = d2 * (1.0 / 0.4)
        env[...] = jnp.square(jnp.maximum(0.0, 1.0 - d2 * (1.0 / 6.0)))
        code = jnp.floor(place * (1.0 / 128.0))
        lo_s[...] = place - code * 128.0
        code_s[...] = code

    def spread_blocks(pair, first, last):
        blocks = (2 * pair, 2 * pair + 1)

        def group(step, _):
            base = pl.multiple_of(step * 8, 8)
            rows = pl.ds(base, 8)
            dz8, env8, lo8, code8 = dz[rows, :], env[rows, :], lo_s[rows, :], code_s[rows, :]
            b_ids = lax.broadcasted_iota(jnp.int32, (NB, 128), 0).astype(F32)
            lo_ids = lax.broadcasted_iota(jnp.int32, (128, 128), 0).astype(F32).astype(BF)
            for s in range(8):
                gap = dz8[s : s + 1, :] - b_ids
                basis = (jnp.exp(-(gap * gap)) * env8[s : s + 1, :]).astype(BF)
                code = jnp.broadcast_to(code8[s : s + 1, :], (NB, 128)).astype(BF)
                lhs = jnp.concatenate(
                    [jnp.where(code == h, basis, jnp.zeros_like(basis)) for h in range(8)], axis=0
                )
                lo = jnp.broadcast_to(lo8[s : s + 1, :], (128, 128)).astype(BF)
                hot = jnp.where(lo_ids == lo, jnp.ones_like(lo), jnp.zeros_like(lo))
                out = nt(lhs, hot).astype(BF)
                for i in range(2):
                    at = pl.multiple_of((blocks[i] * BLOCK + s) * NB + base * NB, NB)
                    for h in range(4):
                        r = (i * 4 + h) * NB
                        gmat[pl.ds(at, NB), h * 128 : h * 128 + 128] = out[r : r + NB, :]
            return 0

        lax.fori_loop(first, last, group, 0)

    spread_setup(0)
    spread_blocks(0, 0, 8)

    cores.wait()

    def add_core(step, _):
        rows = pl.ds(pl.multiple_of(step * 64, 64), 64)
        val = xs[rows, :] + rc[rows, :].astype(F32)
        xs[rows, :] = val
        xs_b[rows, :] = val.astype(BF)
        return 0

    lax.fori_loop(0, KCOUNT // 64, add_core, 0)

    scatters = [
        pltpu.make_async_remote_copy(
            src_ref=xs_b.at[pl.ds(pl.multiple_of(to * PIECE, PIECE), PIECE)], dst_ref=rx.at[i],
            send_sem=rs_send.at[i], recv_sem=rs_recv.at[i], device_id=peer, device_id_type=MESH,
        )
        for i, (to, peer) in enumerate(places)
    ]
    for c in scatters:
        c.start()

    spread_blocks(0, 8, 16)
    spread_setup(1)
    spread_blocks(1, 0, 16)

    for c in scatters:
        c.wait()
    own = xs[pl.ds(pl.multiple_of(chip * PIECE, PIECE), PIECE), :]
    own = lax.fori_loop(0, CHIPS - 1, lambda i, v: v + rx[i].astype(F32), own)
    at_piece = pl.ds(pl.multiple_of(mine + chip * PIECE, PIECE), PIECE)
    at_half = pl.ds(mine, KCOUNT)
    ag[at_piece, :] = own.astype(BF)
    gathers = [
        pltpu.make_async_remote_copy(
            src_ref=ag.at[at_piece], dst_ref=ag.at[at_piece],
            send_sem=ag_send.at[i], recv_sem=ag_recv.at[i], device_id=peer, device_id_type=MESH,
        )
        for i, (_, peer) in enumerate(places)
    ]
    for c in gathers:
        c.start()

    for c in halo:
        c.wait()
    u_own[...] = nn(feat[...], wmsg[...]).astype(BF)
    u_ghost[...] = nn(ghost[...], wmsg[...]).astype(BF)
    gul[...] = jnp.zeros_like(gul)
    gug[...] = jnp.zeros_like(gug)
    radacc[...] = jnp.zeros_like(radacc)
    wr = wrad[...].astype(F32)

    def edge_block(blk, _):
        w = pl.multiple_of(jnp.clip(blk * BLOCK - BLOCK // 2, 0, WIDTH - WINDOW), 64)
        u_win = u_own[pl.ds(w, WINDOW), :]
        ug = u_ghost[...]
        piece = 32

        def atoms(step, _):
            at = pl.multiple_of(blk * BLOCK + step * piece, piece)
            rows = pl.ds(pl.multiple_of(at * NB, NB * piece), NB * piece)
            summed = nn(gmat[rows, :WINDOW], u_win) + nn(gmat[rows, WINDOW:], ug)
            summed = summed.reshape(piece, NB, CHANS)
            pre = jnp.sum(summed * wr[None], axis=1)
            sig = 1.0 / (1.0 + jnp.exp(-pre))
            gpre = fg[pl.ds(at, piece), CHANS:].astype(F32) * sig * (1.0 + pre * (1.0 - sig))
            wide = gpre[:, None, :]
            radacc[...] += jnp.sum(wide * summed, axis=0)
            ymat[pl.ds(pl.multiple_of(step * piece * NB, NB * piece), NB * piece), :] = (
                (wide * wr[None]).reshape(piece * NB, CHANS).astype(BF)
            )
            return 0

        lax.fori_loop(0, BLOCK // piece, atoms, 0)
        rows = pl.ds(pl.multiple_of(blk * BLOCK * NB, BLOCK * NB), BLOCK * NB)
        collected = jnp.transpose(tn(ymat[...], gmat[rows, :]))
        gul[pl.ds(w, WINDOW), :] += collected[:WINDOW, :]
        gug[...] += collected[WINDOW:, :]
        return 0

    lax.fori_loop(0, WIDTH // BLOCK, edge_block, 0)

    gu_g = gug[...].astype(BF)
    gu_l = gul[...].astype(BF)
    gmsg = tn(feat[...], gu_l) + tn(ghost[...], gu_g)

    ar[:, 0:16, :] = gmsg.reshape(8, 16, CHANS)
    ar[:, 16:24, :] = jnp.zeros((8, 8, CHANS), F32)
    for j in range(8):
        ar[j, 16:18, :] = radacc[2 * j : 2 * j + 2, :]
    me = x * 2 + core
    ar_first = []
    for o, peer in enumerate(across):
        ar_first.append(copy(ar.at[lax.rem(peer[0], 32) // 8 * 2 + lax.rem(peer[1], 2)], ar1.at[o], peer))
    for c in ar_first:
        c.start()

    gh_b[...] = nt(gu_g, wmsg[...]).astype(BF)
    returns = [
        copy(gh_b.at[pl.ds(0, GHOSTS)], back.at[pl.ds(GHOSTS, GHOSTS)], lower),
        copy(gh_b.at[pl.ds(GHOSTS, GHOSTS)], back.at[pl.ds(0, GHOSTS)], upper),
    ]
    for c in returns:
        c.start()

    gul[...] = fg[:, CHANS:].astype(F32) + nt(gu_l, wmsg[...])

    for c in gathers:
        c.wait()
    gather_core = copy(ag.at[at_half], ag.at[at_half], other_core)
    gather_core.start()

    def half_of(start, which):
        def flip(step, _):
            at = pl.multiple_of(step * 128, 128)
            base = pl.multiple_of(start + at, 128)
            part = jnp.transpose(ag[pl.ds(base, 128), CHANS:].astype(F32))
            weight = kern[:, pl.ds(at, 128)] * (1.0 / math.sqrt(KCOUNT * TOTAL))
            pc_t[:, pl.ds(at, 128)] = (part * weight).astype(BF)
            return 0

        lax.fori_loop(0, KCOUNT // 128, flip, 0)
        rows = pl.ds(start, KCOUNT)
        m_s[which] = nn(pc_t[...], ag[rows, :CHANS])
        return nn(pc_t[...], table[rows, :])

    p_t[...] = half_of(mine, core)

    for c in ar_first:
        c.wait()
    val = ar[me]
    for o in range(7):
        val = val + ar1[o]
    ar2[yz] = val
    ar_yz = [copy(ar2.at[yz], ar2.at[yz], peer) for _, (_, peer) in plane]
    for c in ar_yz:
        c.start()

    gather_core.wait()
    p_b = (p_t[...] + half_of(theirs, 1 - core)).astype(BF)
    gq_t = nn(wo[...], p_b).astype(BF)
    ghq = jnp.transpose(nn(wq[...], gq_t))
    base_grad = gul[...] + jnp.where(live, ghq, 0.0)
    for c in returns:
        c.wait()
    gf[...] = base_grad + nn(place_t[...], back[...])
    outs = [
        pltpu.make_async_copy(src, dst, out_sem.at[i])
        for i, (src, dst) in enumerate(
            [(gf, gf_out), (gwq, gwq_out), (gwo, gwo_out), (gmsg_s, gmsg_out), (rad_s, rad_out)]
        )
    ]
    outs[0].start()

    rscale = 1.0 / math.sqrt(TOTAL)
    m_full = jnp.transpose(m_s[0] + m_s[1])
    m_hi = m_full.astype(BF)
    m_lo = (m_full - m_hi.astype(F32)).astype(BF)
    gwq[...] = (nt(m_hi, wo[...]) + nt(m_lo, wo[...])) * rscale
    wq_t = transposed(wq[...])
    gwo[...] = (nn(wq_t, m_hi) + nn(wq_t, m_lo)) * rscale
    outs[1].start()
    outs[2].start()

    for c in ar_yz:
        c.wait()
    val = ar2[0]
    for j in range(1, YZ):
        val = val + ar2[j]
    fin[me] = val
    ar_fin = [copy(fin.at[me], fin.at[me], peer) for peer in across]
    for c in ar_fin:
        c.start()
    for c in ar_fin:
        c.wait()
    gmsg_s[...] = fin[:, 0:16, :].reshape(CHANS, CHANS) * rscale
    outs[3].start()
    for j in range(8):
        rad_s[2 * j : 2 * j + 2, :] = fin[j, 16:18, :] * (rscale / math.sqrt(SLOTS))
    outs[4].start()
    for c in outs:
        c.wait()


def finish(*refs):
    ins, outs, held, sem = refs[:5], refs[5:10], refs[10:15], refs[15]
    reads = [pltpu.make_async_copy(ins[i], held[i], sem.at[i]) for i in range(5)]
    writes = [pltpu.make_async_copy(held[i], outs[i], sem.at[5 + i]) for i in range(5)]
    for r in reads:
        r.start()
    for r, w in zip(reads, writes):
        r.wait()
        w.start()
    for w in writes:
        w.wait()


def on_device(features, frac, k_int, kern, dist, nbr, send_index, counts, cot, w_msg, w_rad, w_q, w_o):
    hbm = pl.BlockSpec(memory_space=pltpu.HBM)

    def buf(*shape, dtype=BF):
        return pltpu.VMEM(shape, dtype)

    def result(*shape):
        return jax.ShapeDtypeStruct(shape, F32)

    shapes = (result(WIDTH, CHANS), result(CHANS, CHANS), result(NB, CHANS), result(CHANS, CHANS), result(CHANS, CHANS))
    sums = pl.pallas_call(
        kernel,
        out_shape=shapes,
        in_specs=[hbm] * 13,
        out_specs=(hbm,) * 5,
        scratch_shapes=[
            buf(WIDTH, CHANS),
            buf(3, WIDTH, dtype=F32),
            buf(3, KCOUNT, dtype=jnp.int32),
            buf(1, KCOUNT, dtype=F32),
            buf(SLOTS, WIDTH, dtype=F32),
            buf(SLOTS, WIDTH, dtype=jnp.int32),
            buf(2, GHOSTS, dtype=jnp.int32),
            pltpu.SMEM((1,), jnp.int32),
            buf(WIDTH, CHANS),
            buf(CHANS, CHANS),
            buf(NB, CHANS),
            buf(CHANS, CHANS),
            buf(CHANS, CHANS),
            buf(WIDTH, CHANS, dtype=F32),
            buf(CHANS, CHANS, dtype=F32),
            buf(NB, CHANS, dtype=F32),
            buf(CHANS, CHANS, dtype=F32),
            buf(CHANS, CHANS, dtype=F32),
            buf(2 * KCOUNT, WIDTH),
            buf(KCOUNT, BOTH),
            buf(KCOUNT, BOTH),
            buf(KCOUNT, BOTH, dtype=F32),
            buf(KCOUNT, BOTH),
            buf(CHIPS - 1, PIECE, BOTH),
            buf(2 * KCOUNT, BOTH),
            buf(CHANS, KCOUNT),
            buf(WIDTH, BOTH),
            buf(WIDTH, 2 * GHOSTS),
            buf(2 * GHOSTS, CHANS),
            buf(2 * GHOSTS, CHANS),
            buf(WIDTH, CHANS),
            buf(2 * GHOSTS, CHANS),
            buf(BLOCK, 128, dtype=F32),
            buf(BLOCK, 128, dtype=F32),
            buf(BLOCK, 128, dtype=F32),
            buf(BLOCK, 128, dtype=F32),
            buf(WIDTH * NB, 2 * WINDOW),
            buf(BLOCK * NB, CHANS),
            buf(WIDTH, CHANS, dtype=F32),
            buf(2 * GHOSTS, CHANS, dtype=F32),
            buf(NB, CHANS, dtype=F32),
            buf(2 * GHOSTS, CHANS),
            buf(2 * GHOSTS, CHANS),
            buf(CHANS, WIDTH, dtype=F32),
            buf(2, CHANS, CHANS, dtype=F32),
            buf(8, ROWS_AR, CHANS, dtype=F32),
            buf(7, ROWS_AR, CHANS, dtype=F32),
            buf(YZ, ROWS_AR, CHANS, dtype=F32),
            buf(8, ROWS_AR, CHANS, dtype=F32),
            pltpu.SemaphoreType.DMA((13,)),
            pltpu.SemaphoreType.DMA((5,)),
            pltpu.SemaphoreType.DMA((40,)),
            pltpu.SemaphoreType.DMA((40,)),
            pltpu.SemaphoreType.DMA((CHIPS - 1,)),
            pltpu.SemaphoreType.DMA((CHIPS - 1,)),
            pltpu.SemaphoreType.DMA((CHIPS - 1,)),
            pltpu.SemaphoreType.DMA((CHIPS - 1,)),
        ],
        compiler_params=pltpu.CompilerParams(
            collective_id=0, has_side_effects=True, vmem_limit_bytes=VMEM_BYTES
        ),
        name="ewald_backward",
    )(
        features, frac, k_int, kern.reshape(1, KCOUNT), dist.T, nbr.T,
        send_index.reshape(2, GHOSTS), counts, cot, w_msg, w_rad, w_q, w_o,
    )
    return pl.pallas_call(
        finish,
        out_shape=shapes,
        in_specs=[hbm] * 5,
        out_specs=(hbm,) * 5,
        scratch_shapes=[buf(*t.shape, dtype=F32) for t in shapes] + [pltpu.SemaphoreType.DMA((10,))],
        compiler_params=pltpu.CompilerParams(vmem_limit_bytes=VMEM_BYTES),
        name="finish",
    )(*sums)


def solution(mesh):
    rows = P(("dom", "sub"), None)
    placed = (
        rows, P(None, ("dom", "sub")), P(), P(), rows, rows,
        P(("dom", "sub"), None, None), P(("dom", "sub")), rows, P(), P(), P(), P(),
    )
    return jax.shard_map(
        on_device,
        mesh=mesh,
        in_specs=placed,
        out_specs=(rows, P(), P(), P(), P()),
        check_vma=False,
    )
```

time: 66.7 us -> 52.9 us (0.79)
  Pallas kernels: 60 us -> 51.4 us
  local copies, waits for them, and re-layouts: 5.16 us -> 0 us
    pallas_call x1 -> x2, Pallas kernels: 60 us -> 51.4 us  [the longest x1 49.6 us: on_device(): pl.pallas_call(kernel, out_shape=shapes, in_specs=[hbm] * 13, out_specs=(...]
    unnamed x29 -> x0, local copies, waits for them, and re-layouts: 5.16 us -> none
where the time goes in v1:
time: 52.9 us; the launch traced here: 52.7 us
  Pallas kernels  51.4 us (97%)
  between operations  1.29 us (2%)
    pallas_call x1, Pallas kernels, on_device(): pl.pallas_call(kernel, out_shape=shapes, in_specs=[hbm] * 13, out_specs=(...  49.6 us
    pallas_call x1, Pallas kernels, on_device(): pl.pallas_call(finish, out_shape=shapes, in_specs=[hbm] * 5, out_specs=(h...  1.8 us

profile of v1, /device:TPU:1, one launch (start us, length us, event | category | flops | bytes accessed | tf_op | source)
XLA Modules:
  0.0 52.7 jit_solution(570430823091745600)
XLA Ops:
  1.3 49.6 %ewald_backward.1 = (f32[512,128]{1,0:T(8,128)}, f32[128,128]{1,0:T(8,128)}, f32[16,128]{1,0:T(8,128)}, f32[128,128]{1,0:T(8,128)}, f32[128,128]{1,0:T(8,128)}) custom-call(bf16[512,128]{1,0:T(8,128)(2,1)} %feat_h.1, f32[3,512]{1,0:T(4,128)} %frac_h.1, s32[3,1024]{1,0:T(4,128)} %kint_h.1, f32[1,1024]{1,0:T(1,128)} %bitcast.6, f32[64,512]{1,0:T(8,128)} %bitcast.4, ...), custom_call_target="tpu_custom_call" | custom-call | tf_op jit(solution)/shard_map/ewald_backward/pallas_call | solution.py:431
  50.9 1.8 %finish.1 = (f32[512,128]{1,0:T(8,128)}, f32[128,128]{1,0:T(8,128)}, f32[16,128]{1,0:T(8,128)}, f32[128,128]{1,0:T(8,128)}, f32[128,128]{1,0:T(8,128)}) custom-call(f32[512,128]{1,0:T(8,128)} %get-tuple-element.10.refs_0_, f32[128,128]{1,0:T(8,128)} %get-tuple-element.11.refs_1_, f32[16,128]{1,0:T(8,128)} %get-tuple-element.12.refs_2_, ...), custom_call_target="tpu_custom_call" | custom-call | tf_op jit(solution)/shard_map/finish/pallas_call | solution.py:503

commit v2 on v1

--- a/solution.py
+++ b/solution.py
@@ -17,6 +17,7 @@
 X, YZ, CORES = 4, 16, 2
 CHIPS = X * YZ
 PIECE = KCOUNT // CHIPS
+QUART = KCOUNT // X
 TOTAL = WIDTH * CHIPS * CORES
 BOTH = 2 * CHANS
 ROWS_AR = 24
@@ -61,11 +62,19 @@
     gf_out, gmsg_out, rad_out, gwq_out, gwo_out,
     feat, frac, kint, kern, dist, nbr, send, counts, cot, wmsg, wrad, wq, wo,
     gf, gmsg_s, rad_s, gwq, gwo,
-    table, sg_b, rc, xs, xs_b, rx, ag, pc_t,
+    table, sg_b, rc, xs, xs_b, rx, ag,
     fg, place_t, out_b, ghost, u_own, u_ghost,
-    dz, env, lo_s, code_s, gmat, ymat, gul, gug, radacc, gh_b, back, p_t, m_s,
+    split_k, split_f, dz, env, lo_s, code_s, own_w, gmat, amat, ymat, gul, gug, radacc, gh_b, back, p_t, m_s,
     ar, ar1, ar2, fin, in_sem, out_sem, send_sem, recv_sem, rs_send, rs_recv, ag_send, ag_recv,
 ):
+    pairs = [
+        (kint_h, kint), (frac_h, frac), (counts_h, counts), (feat_h, feat), (cot_h, cot), (send_h, send),
+        (dist_h, dist), (nbr_h, nbr), (wmsg_h, wmsg), (wrad_h, wrad), (kern_h, kern), (wq_h, wq), (wo_h, wo),
+    ]
+    loads = [pltpu.make_async_copy(src, dst, in_sem.at[i]) for i, (src, dst) in enumerate(pairs)]
+    for c in loads:
+        c.start()
+
     dom, sub = lax.axis_index("dom"), lax.axis_index("sub")
     x, zlo, y = dom // 8, (dom // 4) % 2, dom % 4
     zhi, core = sub // 2, sub % 2
@@ -89,10 +98,16 @@
     def hops(turn):
         return sum(min(d, 4 - d) for d in turn)
 
+    steps = (2, 1, 3, 0)
     turns = [(a, b, c) for a in range(4) for b in range(4) for c in range(4) if a or b or c]
-    turns = sorted(turns, key=lambda t: -hops(t))
+    turns = sorted(turns, key=lambda t: (steps.index(t[0]), -hops(t)))
     places = [shifted(*t) for t in turns]
     plane = [(t, p) for t, p in zip(turns, places) if not t[0]]
+    across = [(dx, dc) for dx in (2, 1, 3, 0) for dc in (1, 0) if dx or dc]
+    across = [shifted(dx, 0, 0, dc)[1] for dx, dc in across]
+
+    def group_of(dx):
+        return [i for i, t in enumerate(turns) if t[0] == dx]
 
     other_core = (dom, zhi * 2 + 1 - core)
     upper, lower = (flat + 1) % 128, (flat + 127) % 128
@@ -113,7 +128,7 @@
         greet(shifted(dx, 0, 0, 1)[1])
     greeted = CHIPS - 1 + 3 + X - 1
 
-    sems = iter(range(128))
+    sems = iter(range(48))
 
     def copy(src, dst, peer):
         at = next(sems)
@@ -122,61 +137,74 @@
             device_id=peer, device_id_type=MESH,
         )
 
-    pairs = [
-        (counts_h, counts), (kint_h, kint), (frac_h, frac), (feat_h, feat), (cot_h, cot), (send_h, send),
-        (dist_h, dist), (nbr_h, nbr), (wmsg_h, wmsg), (wrad_h, wrad), (kern_h, kern), (wq_h, wq), (wo_h, wo),
-    ]
-    loads = [pltpu.make_async_copy(src, dst, in_sem.at[i]) for i, (src, dst) in enumerate(pairs)]
-    for c in loads:
-        c.start()
-    for c in loads:
-        c.wait()
-
+    loads[0].wait()
+    loads[1].wait()
+    part = frac[...]
+    blank = jnp.zeros((5, WIDTH), F32)
+    pieces = []
+    for _ in range(3):
+        high = part.astype(BF).astype(F32)
+        pieces += [high, blank]
+        part = part - high
+    split_f[...] = jnp.concatenate(pieces + [jnp.zeros((8, WIDTH), F32)], axis=0).astype(BF)
+    k_rows = jnp.concatenate([kint[...].astype(F32), jnp.zeros((5, KCOUNT), F32)], axis=0)
+    split_k[...] = jnp.concatenate([k_rows] * 3 + [jnp.zeros((8, KCOUNT), F32)], axis=0).astype(BF)
+
+    def table_rows(step, _):
+        base = pl.multiple_of(step * 256, 256)
+        ks = split_k[:, pl.ds(base, 256)]
+        for block in range(4):
+            cols = slice(block * 128, block * 128 + 128)
+            turns = tn(ks, split_f[:, cols])
+            turns = turns - jnp.floor(turns + 0.5)
+            square = turns * turns
+            table[pl.ds(base, 256), cols] = horner(COS, square).astype(BF)
+            table[pl.ds(KCOUNT + base, 256), cols] = (horner(SIN, square) * turns).astype(BF)
+        return 0
+
+    lax.fori_loop(0, KCOUNT // 256, table_rows, 0)
+
+    for c in loads[2:5]:
+        c.wait()
     live = lax.broadcasted_iota(jnp.int32, (WIDTH, CHANS), 0) < counts[0]
     fg[:, :CHANS] = jnp.where(live, feat[...].astype(F32), 0.0).astype(BF)
     fg[:, CHANS:] = jnp.where(live, cot[...].astype(F32), 0.0).astype(BF)
+    theirs = pl.multiple_of((1 - core) * KCOUNT, KCOUNT)
+    mine = pl.multiple_of(core * KCOUNT, KCOUNT)
+    sg_b[...] = nn(table[pl.ds(theirs, KCOUNT), :], fg[...]).astype(BF)
+    xs[...] = nn(table[pl.ds(mine, KCOUNT), :], fg[...])
+
+    loads[5].wait()
     picks = jnp.concatenate([send[0:1, :], send[1:2, :]], axis=1)
     place_t[...] = jnp.where(
         lax.broadcasted_iota(jnp.int32, (WIDTH, 2 * GHOSTS), 0) == picks, 1.0, 0.0
     ).astype(BF)
     out_b[...] = tn(place_t[...], feat[...]).astype(BF)
 
-    def table_rows(step, _):
-        base = pl.multiple_of(step * 128, 128)
-        k_real = kint[:, pl.ds(base, 128)].astype(F32)
-        for part in range(4):
-            cols = slice(part * 128, part * 128 + 128)
-            turns = lax.dot_general(
-                k_real, frac[:, cols], (((0,), (0,)), ((), ())),
-                precision=lax.Precision.HIGHEST, preferred_element_type=F32,
-            )
-            turns = turns - jnp.floor(turns + 0.5)
-            square = turns * turns
-            table[pl.ds(base, 128), cols] = horner(COS, square).astype(BF)
-            table[pl.ds(KCOUNT + base, 128), cols] = (horner(SIN, square) * turns).astype(BF)
-        return 0
-
-    lax.fori_loop(0, KCOUNT // 128, table_rows, 0)
-
-    theirs = pl.multiple_of((1 - core) * KCOUNT, KCOUNT)
-    mine = pl.multiple_of(core * KCOUNT, KCOUNT)
-    sg_b[...] = nn(table[pl.ds(theirs, KCOUNT), :], fg[...]).astype(BF)
-    xs[...] = nn(table[pl.ds(mine, KCOUNT), :], fg[...])
-
     pl.semaphore_wait(barrier, greeted)
 
     halo = [
         copy(out_b.at[pl.ds(0, GHOSTS)], ghost.at[pl.ds(GHOSTS, GHOSTS)], lower),
         copy(out_b.at[pl.ds(GHOSTS, GHOSTS)], ghost.at[pl.ds(0, GHOSTS)], upper),
     ]
-    cores = copy(sg_b, rc, other_core)
-    for c in [cores] + halo:
-        c.start()
+    quarters = [pl.ds(pl.multiple_of(px[dx] * QUART, QUART), QUART) for dx in range(4)]
+    cores = [copy(sg_b.at[quarters[dx]], rc.at[quarters[dx]], other_core) for dx in steps]
+    for c in cores[:2] + halo + cores[2:]:
+        c.start()
+    scatters = [
+        pltpu.make_async_remote_copy(
+            src_ref=xs_b.at[pl.ds(pl.multiple_of(to * PIECE, PIECE), PIECE)], dst_ref=rx.at[i],
+            send_sem=rs_send.at[i], recv_sem=rs_recv.at[i], device_id=peer, device_id_type=MESH,
+        )
+        for i, (to, peer) in enumerate(places)
+    ]
+    for c in loads[6:]:
+        c.wait()
 
     def spread_setup(pair):
-        blocks = (2 * pair, 2 * pair + 1)
         d_parts, p_parts = [], []
-        for i, blk in enumerate(blocks):
+        for i in range(2):
+            blk = 2 * pair + i
             w = min(max(blk * BLOCK - BLOCK // 2, 0), WIDTH - WINDOW)
             cols = slice(blk * BLOCK, (blk + 1) * BLOCK)
             n = nbr[:, cols]
@@ -184,124 +212,109 @@
             place = jnp.where(n >= WIDTH, n - (WIDTH - WINDOW), n - w) + i * 2 * WINDOW
             p_parts.append(place.astype(F32))
         d2 = jnp.transpose(jnp.concatenate(d_parts, axis=0))
-        place = jnp.transpose(jnp.concatenate(p_parts, axis=0))
-        dz[...] = d2 * (1.0 / 0.4)
-        env[...] = jnp.square(jnp.maximum(0.0, 1.0 - d2 * (1.0 / 6.0)))
+        place = jnp.concatenate(p_parts, axis=0)
         code = jnp.floor(place * (1.0 / 128.0))
-        lo_s[...] = place - code * 128.0
-        code_s[...] = code
-
-    def spread_blocks(pair, first, last):
-        blocks = (2 * pair, 2 * pair + 1)
+        dz[pair] = d2 * (1.0 / 0.4)
+        env[pair] = jnp.square(jnp.maximum(0.0, 1.0 - d2 * (1.0 / 6.0)))
+        lo_s[pair] = place - code * 128.0
+        code_s[pair] = jnp.transpose(code)
+
+    def spread_blocks(pair):
+        many = 64
 
         def group(step, _):
-            base = pl.multiple_of(step * 8, 8)
-            rows = pl.ds(base, 8)
-            dz8, env8, lo8, code8 = dz[rows, :], env[rows, :], lo_s[rows, :], code_s[rows, :]
+            base = pl.multiple_of(step * many, many)
+            rows = pl.ds(base, many)
+            dz_r, env_r, code_r = dz[pair, rows, :], env[pair, rows, :], code_s[pair, rows, :]
+            lo_c = pltpu.roll(lo_s[pair], lax.rem(BLOCK - base, BLOCK), 1)
             b_ids = lax.broadcasted_iota(jnp.int32, (NB, 128), 0).astype(F32)
-            lo_ids = lax.broadcasted_iota(jnp.int32, (128, 128), 0).astype(F32).astype(BF)
-            for s in range(8):
-                gap = dz8[s : s + 1, :] - b_ids
-                basis = (jnp.exp(-(gap * gap)) * env8[s : s + 1, :]).astype(BF)
-                code = jnp.broadcast_to(code8[s : s + 1, :], (NB, 128)).astype(BF)
+            lane = lax.broadcasted_iota(jnp.int32, (128, 128), 1).astype(F32).astype(BF)
+            one, zero = jnp.ones((128, 128), BF), jnp.zeros((128, 128), BF)
+            for s in range(many):
+                gap = dz_r[s : s + 1, :] - b_ids
+                basis = (jnp.exp(-(gap * gap)) * env_r[s : s + 1, :]).astype(BF)
+                code = jnp.broadcast_to(code_r[s : s + 1, :], (NB, 128)).astype(BF)
                 lhs = jnp.concatenate(
                     [jnp.where(code == h, basis, jnp.zeros_like(basis)) for h in range(8)], axis=0
                 )
-                lo = jnp.broadcast_to(lo8[s : s + 1, :], (128, 128)).astype(BF)
-                hot = jnp.where(lo_ids == lo, jnp.ones_like(lo), jnp.zeros_like(lo))
-                out = nt(lhs, hot).astype(BF)
+                low = jnp.broadcast_to(lo_c[:, s : s + 1], (128, 128)).astype(BF)
+                out = nn(lhs, jnp.where(lane == low, one, zero)).astype(BF)
                 for i in range(2):
-                    at = pl.multiple_of((blocks[i] * BLOCK + s) * NB + base * NB, NB)
+                    at = pl.multiple_of(((2 * pair + i) * BLOCK + s) * NB + base * NB, NB)
                     for h in range(4):
                         r = (i * 4 + h) * NB
                         gmat[pl.ds(at, NB), h * 128 : h * 128 + 128] = out[r : r + NB, :]
             return 0
 
-        lax.fori_loop(first, last, group, 0)
+        lax.fori_loop(0, BLOCK // many, group, 0)
 
     spread_setup(0)
-    spread_blocks(0, 0, 8)
-
-    cores.wait()
-
-    def add_core(step, _):
-        rows = pl.ds(pl.multiple_of(step * 64, 64), 64)
-        val = xs[rows, :] + rc[rows, :].astype(F32)
-        xs[rows, :] = val
-        xs_b[rows, :] = val.astype(BF)
-        return 0
-
-    lax.fori_loop(0, KCOUNT // 64, add_core, 0)
-
-    scatters = [
-        pltpu.make_async_remote_copy(
-            src_ref=xs_b.at[pl.ds(pl.multiple_of(to * PIECE, PIECE), PIECE)], dst_ref=rx.at[i],
-            send_sem=rs_send.at[i], recv_sem=rs_recv.at[i], device_id=peer, device_id_type=MESH,
-        )
-        for i, (to, peer) in enumerate(places)
-    ]
-    for c in scatters:
-        c.start()
-
-    spread_blocks(0, 8, 16)
     spread_setup(1)
-    spread_blocks(1, 0, 16)
-
-    for c in scatters:
-        c.wait()
-    own = xs[pl.ds(pl.multiple_of(chip * PIECE, PIECE), PIECE), :]
-    own = lax.fori_loop(0, CHIPS - 1, lambda i, v: v + rx[i].astype(F32), own)
-    at_piece = pl.ds(pl.multiple_of(mine + chip * PIECE, PIECE), PIECE)
-    at_half = pl.ds(mine, KCOUNT)
-    ag[at_piece, :] = own.astype(BF)
-    gathers = [
-        pltpu.make_async_remote_copy(
-            src_ref=ag.at[at_piece], dst_ref=ag.at[at_piece],
-            send_sem=ag_send.at[i], recv_sem=ag_recv.at[i], device_id=peer, device_id_type=MESH,
-        )
-        for i, (_, peer) in enumerate(places)
-    ]
-    for c in gathers:
-        c.start()
-
-    for c in halo:
-        c.wait()
+
+    weights = kern[...] * (1.0 / math.sqrt(KCOUNT * TOTAL))
+    weights = pltpu.roll(weights, lax.rem(KCOUNT - chip * PIECE, KCOUNT), 1)[:, :CHANS]
+    own_w[...] = jnp.transpose(jnp.broadcast_to(weights, (CHANS, CHANS)))[:PIECE, :]
+
+    for dx, c in zip(steps, cores):
+        c.wait()
+        val = xs[quarters[dx], :] + rc[quarters[dx], :].astype(F32)
+        xs_b[quarters[dx], :] = val.astype(BF)
+        if not dx:
+            xs[quarters[dx], :] = val
+        for i in group_of(dx):
+            scatters[i].start()
+
+    spread_blocks(0)
+    spread_blocks(1)
+
     u_own[...] = nn(feat[...], wmsg[...]).astype(BF)
-    u_ghost[...] = nn(ghost[...], wmsg[...]).astype(BF)
     gul[...] = jnp.zeros_like(gul)
     gug[...] = jnp.zeros_like(gug)
     radacc[...] = jnp.zeros_like(radacc)
     wr = wrad[...].astype(F32)
 
-    def edge_block(blk, _):
-        w = pl.multiple_of(jnp.clip(blk * BLOCK - BLOCK // 2, 0, WIDTH - WINDOW), 64)
-        u_win = u_own[pl.ds(w, WINDOW), :]
-        ug = u_ghost[...]
+    def window_of(blk):
+        return pl.ds(min(max(blk * BLOCK - BLOCK // 2, 0), WIDTH - WINDOW), WINDOW)
+
+    def rows_of(blk):
+        return pl.ds(blk * BLOCK * NB, BLOCK * NB)
+
+    blocks = WIDTH // BLOCK
+    for blk in range(blocks):
+        amat[rows_of(blk), :] = nn(gmat[rows_of(blk), :WINDOW], u_own[window_of(blk), :])
+    for c in halo:
+        c.wait()
+    u_ghost[...] = nn(ghost[...], wmsg[...]).astype(BF)
+
+    def gathered(blk):
+        amat[rows_of(blk), :] += nn(gmat[rows_of(blk), WINDOW:], u_ghost[...])
+
+    def atoms(blk):
         piece = 32
-
-        def atoms(step, _):
-            at = pl.multiple_of(blk * BLOCK + step * piece, piece)
-            rows = pl.ds(pl.multiple_of(at * NB, NB * piece), NB * piece)
-            summed = nn(gmat[rows, :WINDOW], u_win) + nn(gmat[rows, WINDOW:], ug)
-            summed = summed.reshape(piece, NB, CHANS)
+        for step in range(BLOCK // piece):
+            at = blk * BLOCK + step * piece
+            rows = pl.ds(at * NB, piece * NB)
+            summed = amat[rows, :].reshape(piece, NB, CHANS)
             pre = jnp.sum(summed * wr[None], axis=1)
             sig = 1.0 / (1.0 + jnp.exp(-pre))
             gpre = fg[pl.ds(at, piece), CHANS:].astype(F32) * sig * (1.0 + pre * (1.0 - sig))
             wide = gpre[:, None, :]
             radacc[...] += jnp.sum(wide * summed, axis=0)
-            ymat[pl.ds(pl.multiple_of(step * piece * NB, NB * piece), NB * piece), :] = (
-                (wide * wr[None]).reshape(piece * NB, CHANS).astype(BF)
-            )
-            return 0
-
-        lax.fori_loop(0, BLOCK // piece, atoms, 0)
-        rows = pl.ds(pl.multiple_of(blk * BLOCK * NB, BLOCK * NB), BLOCK * NB)
-        collected = jnp.transpose(tn(ymat[...], gmat[rows, :]))
-        gul[pl.ds(w, WINDOW), :] += collected[:WINDOW, :]
+            ymat[rows, :] = (wide * wr[None]).reshape(piece * NB, CHANS).astype(BF)
+
+    def scattered(blk):
+        collected = jnp.transpose(tn(ymat[rows_of(blk), :], gmat[rows_of(blk), :]))
+        gul[window_of(blk), :] += collected[:WINDOW, :]
         gug[...] += collected[WINDOW:, :]
-        return 0
-
-    lax.fori_loop(0, WIDTH // BLOCK, edge_block, 0)
+
+    gathered(0)
+    for blk in range(blocks):
+        if blk + 1 < blocks:
+            gathered(blk + 1)
+        atoms(blk)
+        if blk:
+            scattered(blk - 1)
+    scattered(blocks - 1)
 
     gu_g = gug[...].astype(BF)
     gu_l = gul[...].astype(BF)
@@ -328,26 +341,23 @@
 
     gul[...] = fg[:, CHANS:].astype(F32) + nt(gu_l, wmsg[...])
 
+    for c in scatters:
+        c.wait()
+    own = xs[pl.ds(pl.multiple_of(chip * PIECE, PIECE), PIECE), :]
+    own = lax.fori_loop(0, CHIPS - 1, lambda i, v: v + rx[i].astype(F32), own)
+    at_piece = pl.ds(pl.multiple_of(mine + chip * PIECE, PIECE), PIECE)
+    ag[at_piece, :CHANS] = own[:, :CHANS].astype(BF)
+    ag[at_piece, CHANS:] = (own[:, CHANS:] * own_w[...]).astype(BF)
+    gathers = [
+        pltpu.make_async_remote_copy(
+            src_ref=ag.at[at_piece], dst_ref=ag.at[at_piece],
+            send_sem=ag_send.at[i], recv_sem=ag_recv.at[i], device_id=peer, device_id_type=MESH,
+        )
+        for i, (_, peer) in enumerate(places)
+    ]
     for c in gathers:
-        c.wait()
-    gather_core = copy(ag.at[at_half], ag.at[at_half], other_core)
-    gather_core.start()
-
-    def half_of(start, which):
-        def flip(step, _):
-            at = pl.multiple_of(step * 128, 128)
-            base = pl.multiple_of(start + at, 128)
-            part = jnp.transpose(ag[pl.ds(base, 128), CHANS:].astype(F32))
-            weight = kern[:, pl.ds(at, 128)] * (1.0 / math.sqrt(KCOUNT * TOTAL))
-            pc_t[:, pl.ds(at, 128)] = (part * weight).astype(BF)
-            return 0
-
-        lax.fori_loop(0, KCOUNT // 128, flip, 0)
-        rows = pl.ds(start, KCOUNT)
-        m_s[which] = nn(pc_t[...], ag[rows, :CHANS])
-        return nn(pc_t[...], table[rows, :])
-
-    p_t[...] = half_of(mine, core)
+        c.start()
+
 
     for c in ar_first:
         c.wait()
@@ -359,7 +369,32 @@
     for c in ar_yz:
         c.start()
 
-    gather_core.wait()
+    for c in ar_yz:
+        c.wait()
+    val = ar2[0]
+    for j in range(1, YZ):
+        val = val + ar2[j]
+    fin[me] = val
+    ar_fin = [copy(fin.at[me], fin.at[me], peer) for peer in across]
+    for c in ar_fin:
+        c.start()
+    passed = []
+    for dx in steps:
+        for i in group_of(dx):
+            gathers[i].wait()
+        rows = pl.ds(pl.multiple_of(mine + px[(4 - dx) % 4] * QUART, QUART), QUART)
+        passed.append(copy(ag.at[rows], ag.at[rows], other_core))
+        passed[-1].start()
+
+    def half_of(start, which):
+        rows = pl.ds(start, KCOUNT)
+        weighted = ag[rows, CHANS:]
+        m_s[which] = tn(weighted, ag[rows, :CHANS])
+        return tn(weighted, table[rows, :])
+
+    p_t[...] = half_of(mine, core)
+    for c in passed:
+        c.wait()
     p_b = (p_t[...] + half_of(theirs, 1 - core)).astype(BF)
     gq_t = nn(wo[...], p_b).astype(BF)
     ghq = jnp.transpose(nn(wq[...], gq_t))
@@ -385,15 +420,6 @@
     outs[1].start()
     outs[2].start()
 
-    for c in ar_yz:
-        c.wait()
-    val = ar2[0]
-    for j in range(1, YZ):
-        val = val + ar2[j]
-    fin[me] = val
-    ar_fin = [copy(fin.at[me], fin.at[me], peer) for peer in across]
-    for c in ar_fin:
-        c.start()
     for c in ar_fin:
         c.wait()
     gmsg_s[...] = fin[:, 0:16, :].reshape(CHANS, CHANS) * rscale
@@ -459,19 +485,22 @@
             buf(KCOUNT, BOTH),
             buf(CHIPS - 1, PIECE, BOTH),
             buf(2 * KCOUNT, BOTH),
-            buf(CHANS, KCOUNT),
             buf(WIDTH, BOTH),
             buf(WIDTH, 2 * GHOSTS),
             buf(2 * GHOSTS, CHANS),
             buf(2 * GHOSTS, CHANS),
             buf(WIDTH, CHANS),
             buf(2 * GHOSTS, CHANS),
-            buf(BLOCK, 128, dtype=F32),
-            buf(BLOCK, 128, dtype=F32),
-            buf(BLOCK, 128, dtype=F32),
-            buf(BLOCK, 128, dtype=F32),
+            buf(32, KCOUNT),
+            buf(32, WIDTH),
+            buf(2, BLOCK, 128, dtype=F32),
+            buf(2, BLOCK, 128, dtype=F32),
+            buf(2, BLOCK, 128, dtype=F32),
+            buf(2, BLOCK, 128, dtype=F32),
+            buf(PIECE, CHANS, dtype=F32),
             buf(WIDTH * NB, 2 * WINDOW),
-            buf(BLOCK * NB, CHANS),
+            buf(WIDTH * NB, CHANS, dtype=F32),
+            buf(WIDTH * NB, CHANS),
             buf(WIDTH, CHANS, dtype=F32),
             buf(2 * GHOSTS, CHANS, dtype=F32),
             buf(NB, CHANS, dtype=F32),
@@ -485,8 +514,8 @@
             buf(8, ROWS_AR, CHANS, dtype=F32),
             pltpu.SemaphoreType.DMA((13,)),
             pltpu.SemaphoreType.DMA((5,)),
-            pltpu.SemaphoreType.DMA((40,)),
-            pltpu.SemaphoreType.DMA((40,)),
+            pltpu.SemaphoreType.DMA((48,)),
+            pltpu.SemaphoreType.DMA((48,)),
             pltpu.SemaphoreType.DMA((CHIPS - 1,)),
             pltpu.SemaphoreType.DMA((CHIPS - 1,)),
             pltpu.SemaphoreType.DMA((CHIPS - 1,)),

time: 52.9 us -> 44.4 us (0.84)
  Pallas kernels: 51.4 us -> 43 us
    pallas_call x1, Pallas kernels: 49.6 us -> 41.2 us  [on_device(): pl.pallas_call(kernel, out_shape=shapes, in_specs=[hbm] * 13, out_specs=(...]
where the time goes in v2:
time: 44.4 us; the launch traced here: 44.3 us
  Pallas kernels  43 us (97%)
  between operations  1.29 us (3%)
    pallas_call x1, Pallas kernels, on_device(): pl.pallas_call(kernel, out_shape=shapes, in_specs=[hbm] * 13, out_specs=(...  41.2 us
    pallas_call x1, Pallas kernels, on_device(): pl.pallas_call(finish, out_shape=shapes, in_specs=[hbm] * 5, out_specs=(h...  1.8 us

profile of v2, /device:TPU:1, one launch (start us, length us, event | category | flops | bytes accessed | tf_op | source)
XLA Modules:
  0.0 44.3 jit_solution(18262955592855719471)
XLA Ops:
  1.3 41.2 %ewald_backward.1 = (f32[512,128]{1,0:T(8,128)}, f32[128,128]{1,0:T(8,128)}, f32[16,128]{1,0:T(8,128)}, f32[128,128]{1,0:T(8,128)}, f32[128,128]{1,0:T(8,128)}) custom-call(bf16[512,128]{1,0:T(8,128)(2,1)} %feat_h.1, f32[3,512]{1,0:T(4,128)} %frac_h.1, s32[3,1024]{1,0:T(4,128)} %kint_h.1, f32[1,1024]{1,0:T(1,128)} %bitcast.6, f32[64,512]{1,0:T(8,128)} %bitcast.4, ...), custom_call_target="tpu_custom_call" | custom-call | tf_op jit(solution)/shard_map/ewald_backward/pallas_call | solution.py:457
  42.5 1.8 %finish.1 = (f32[512,128]{1,0:T(8,128)}, f32[128,128]{1,0:T(8,128)}, f32[16,128]{1,0:T(8,128)}, f32[128,128]{1,0:T(8,128)}, f32[128,128]{1,0:T(8,128)}) custom-call(f32[512,128]{1,0:T(8,128)} %get-tuple-element.10.refs_0_, f32[128,128]{1,0:T(8,128)} %get-tuple-element.11.refs_1_, f32[16,128]{1,0:T(8,128)} %get-tuple-element.12.refs_2_, ...), custom_call_target="tpu_custom_call" | custom-call | tf_op jit(solution)/shard_map/finish/pallas_call | solution.py:532

commit v3 on v2

--- a/solution.py
+++ b/solution.py
@@ -30,7 +30,7 @@
     return [float(np.float32(c)) for c in series.convert(kind=np.polynomial.Polynomial).coef]
 
 
-COS = fitted(lambda y: np.cos(2 * np.pi * np.sqrt(y)), 6)
+COS = fitted(lambda y: np.cos(2 * np.pi * np.sqrt(y)), 5)
 SIN = fitted(lambda y: np.sin(2 * np.pi * np.sqrt(y)) / np.sqrt(y), 5)
 
 
@@ -219,11 +219,12 @@
         lo_s[pair] = place - code * 128.0
         code_s[pair] = jnp.transpose(code)
 
-    def spread_blocks(pair):
+    def spread_blocks(first, last):
         many = 64
 
         def group(step, _):
-            base = pl.multiple_of(step * many, many)
+            pair = step // 2
+            base = pl.multiple_of(step % 2 * many, many)
             rows = pl.ds(base, many)
             dz_r, env_r, code_r = dz[pair, rows, :], env[pair, rows, :], code_s[pair, rows, :]
             lo_c = pltpu.roll(lo_s[pair], lax.rem(BLOCK - base, BLOCK), 1)
@@ -240,13 +241,13 @@
                 low = jnp.broadcast_to(lo_c[:, s : s + 1], (128, 128)).astype(BF)
                 out = nn(lhs, jnp.where(lane == low, one, zero)).astype(BF)
                 for i in range(2):
-                    at = pl.multiple_of(((2 * pair + i) * BLOCK + s) * NB + base * NB, NB)
+                    at = pl.multiple_of((2 * pair + i) * BLOCK * NB + base * NB + s * NB, NB)
                     for h in range(4):
                         r = (i * 4 + h) * NB
                         gmat[pl.ds(at, NB), h * 128 : h * 128 + 128] = out[r : r + NB, :]
             return 0
 
-        lax.fori_loop(0, BLOCK // many, group, 0)
+        lax.fori_loop(first, last, group, 0)
 
     spread_setup(0)
     spread_setup(1)
@@ -254,6 +255,8 @@
     weights = kern[...] * (1.0 / math.sqrt(KCOUNT * TOTAL))
     weights = pltpu.roll(weights, lax.rem(KCOUNT - chip * PIECE, KCOUNT), 1)[:, :CHANS]
     own_w[...] = jnp.transpose(jnp.broadcast_to(weights, (CHANS, CHANS)))[:PIECE, :]
+
+    spread_blocks(0, 1)
 
     for dx, c in zip(steps, cores):
         c.wait()
@@ -264,8 +267,7 @@
         for i in group_of(dx):
             scatters[i].start()
 
-    spread_blocks(0)
-    spread_blocks(1)
+    spread_blocks(1, 4)
 
     u_own[...] = nn(feat[...], wmsg[...]).astype(BF)
     gul[...] = jnp.zeros_like(gul)
@@ -344,7 +346,12 @@
     for c in scatters:
         c.wait()
     own = xs[pl.ds(pl.multiple_of(chip * PIECE, PIECE), PIECE), :]
-    own = lax.fori_loop(0, CHIPS - 1, lambda i, v: v + rx[i].astype(F32), own)
+    def add_some(step, total):
+        for j in range(9):
+            total = total + rx[step * 9 + j].astype(F32)
+        return total
+
+    own = lax.fori_loop(0, (CHIPS - 1) // 9, add_some, own)
     at_piece = pl.ds(pl.multiple_of(mine + chip * PIECE, PIECE), PIECE)
     ag[at_piece, :CHANS] = own[:, :CHANS].astype(BF)
     ag[at_piece, CHANS:] = (own[:, CHANS:] * own_w[...]).astype(BF)

time: 44.4 us -> 43.4 us (0.977)
  Pallas kernels: 43 us -> 42 us
    pallas_call x1, Pallas kernels: 41.2 us -> 40.2 us  [on_device(): pl.pallas_call(kernel, out_shape=shapes, in_specs=[hbm] * 13, out_specs=(...]
where the time goes in v3:
time: 43.4 us; the launch traced here: 43.2 us
  Pallas kernels  42 us (97%)
  between operations  1.29 us (3%)
    pallas_call x1, Pallas kernels, on_device(): pl.pallas_call(kernel, out_shape=shapes, in_specs=[hbm] * 13, out_specs=(...  40.2 us
    pallas_call x1, Pallas kernels, on_device(): pl.pallas_call(finish, out_shape=shapes, in_specs=[hbm] * 5, out_specs=(h...  1.8 us

profile of v3, /device:TPU:1, one launch (start us, length us, event | category | flops | bytes accessed | tf_op | source)
XLA Modules:
  0.0 43.2 jit_solution(6794481531092019905)
XLA Ops:
  1.3 40.2 %ewald_backward.1 = (f32[512,128]{1,0:T(8,128)}, f32[128,128]{1,0:T(8,128)}, f32[16,128]{1,0:T(8,128)}, f32[128,128]{1,0:T(8,128)}, f32[128,128]{1,0:T(8,128)}) custom-call(bf16[512,128]{1,0:T(8,128)(2,1)} %feat_h.1, f32[3,512]{1,0:T(4,128)} %frac_h.1, s32[3,1024]{1,0:T(4,128)} %kint_h.1, f32[1,1024]{1,0:T(1,128)} %bitcast.6, f32[64,512]{1,0:T(8,128)} %bitcast.4, ...), custom_call_target="tpu_custom_call" | custom-call | tf_op jit(solution)/shard_map/ewald_backward/pallas_call | solution.py:464
  41.4 1.8 %finish.1 = (f32[512,128]{1,0:T(8,128)}, f32[128,128]{1,0:T(8,128)}, f32[16,128]{1,0:T(8,128)}, f32[128,128]{1,0:T(8,128)}, f32[128,128]{1,0:T(8,128)}) custom-call(f32[512,128]{1,0:T(8,128)} %get-tuple-element.10.refs_0_, f32[128,128]{1,0:T(8,128)} %get-tuple-element.11.refs_1_, f32[16,128]{1,0:T(8,128)} %get-tuple-element.12.refs_2_, ...), custom_call_target="tpu_custom_call" | custom-call | tf_op jit(solution)/shard_map/finish/pallas_call | solution.py:539

commit v4 on v3

--- a/solution.py
+++ b/solution.py
@@ -371,17 +371,17 @@
     val = ar[me]
     for o in range(7):
         val = val + ar1[o]
-    ar2[yz] = val
+    ar2[yz] = jnp.concatenate([val, jnp.zeros((8, CHANS), F32)], axis=0).astype(BF)
     ar_yz = [copy(ar2.at[yz], ar2.at[yz], peer) for _, (_, peer) in plane]
     for c in ar_yz:
         c.start()
 
     for c in ar_yz:
         c.wait()
-    val = ar2[0]
+    val = ar2[0].astype(F32)
     for j in range(1, YZ):
-        val = val + ar2[j]
-    fin[me] = val
+        val = val + ar2[j].astype(F32)
+    fin[me] = val.astype(BF)
     ar_fin = [copy(fin.at[me], fin.at[me], peer) for peer in across]
     for c in ar_fin:
         c.start()
@@ -429,10 +429,10 @@
 
     for c in ar_fin:
         c.wait()
-    gmsg_s[...] = fin[:, 0:16, :].reshape(CHANS, CHANS) * rscale
+    gmsg_s[...] = fin[:, 0:16, :].astype(F32).reshape(CHANS, CHANS) * rscale
     outs[3].start()
     for j in range(8):
-        rad_s[2 * j : 2 * j + 2, :] = fin[j, 16:18, :] * (rscale / math.sqrt(SLOTS))
+        rad_s[2 * j : 2 * j + 2, :] = fin[j, 16:32, :].astype(F32)[0:2, :] * (rscale / math.sqrt(SLOTS))
     outs[4].start()
     for c in outs:
         c.wait()
@@ -517,8 +517,8 @@
             buf(2, CHANS, CHANS, dtype=F32),
             buf(8, ROWS_AR, CHANS, dtype=F32),
             buf(7, ROWS_AR, CHANS, dtype=F32),
-            buf(YZ, ROWS_AR, CHANS, dtype=F32),
-            buf(8, ROWS_AR, CHANS, dtype=F32),
+            buf(YZ, 32, CHANS),
+            buf(8, 32, CHANS),
             pltpu.SemaphoreType.DMA((13,)),
             pltpu.SemaphoreType.DMA((5,)),
             pltpu.SemaphoreType.DMA((48,)),

time: 43.4 us -> 42.9 us (0.988)
  Pallas kernels: 42 us -> 41.5 us
    pallas_call x1, Pallas kernels: 40.2 us -> 39.7 us  [on_device(): pl.pallas_call(kernel, out_shape=shapes, in_specs=[hbm] * 13, out_specs=(...]
where the time goes in v4:
time: 42.9 us; the launch traced here: 42.8 us
  Pallas kernels  41.5 us (97%)
  between operations  1.29 us (3%)
    pallas_call x1, Pallas kernels, on_device(): pl.pallas_call(kernel, out_shape=shapes, in_specs=[hbm] * 13, out_specs=(...  39.7 us
    pallas_call x1, Pallas kernels, on_device(): pl.pallas_call(finish, out_shape=shapes, in_specs=[hbm] * 5, out_specs=(h...  1.8 us

profile of v4, /device:TPU:1, one launch (start us, length us, event | category | flops | bytes accessed | tf_op | source)
XLA Modules:
  0.0 42.8 jit_solution(6937969836194910355)
XLA Ops:
  1.3 39.7 %ewald_backward.1 = (f32[512,128]{1,0:T(8,128)}, f32[128,128]{1,0:T(8,128)}, f32[16,128]{1,0:T(8,128)}, f32[128,128]{1,0:T(8,128)}, f32[128,128]{1,0:T(8,128)}) custom-call(bf16[512,128]{1,0:T(8,128)(2,1)} %feat_h.1, f32[3,512]{1,0:T(4,128)} %frac_h.1, s32[3,1024]{1,0:T(4,128)} %kint_h.1, f32[1,1024]{1,0:T(1,128)} %bitcast.6, f32[64,512]{1,0:T(8,128)} %bitcast.4, ...), custom_call_target="tpu_custom_call" | custom-call | tf_op jit(solution)/shard_map/ewald_backward/pallas_call | solution.py:464
  41.0 1.8 %finish.1 = (f32[512,128]{1,0:T(8,128)}, f32[128,128]{1,0:T(8,128)}, f32[16,128]{1,0:T(8,128)}, f32[128,128]{1,0:T(8,128)}, f32[128,128]{1,0:T(8,128)}) custom-call(f32[512,128]{1,0:T(8,128)} %get-tuple-element.10.refs_0_, f32[128,128]{1,0:T(8,128)} %get-tuple-element.11.refs_1_, f32[16,128]{1,0:T(8,128)} %get-tuple-element.12.refs_2_, ...), custom_call_target="tpu_custom_call" | custom-call | tf_op jit(solution)/shard_map/finish/pallas_call | solution.py:539
